TPU v7x, 512 devices: a whole 4x8x8 slice. The times are simulated.
512 devices in a mesh: dp: 128 (over x, z, y_hi), grp: 4 (over y_lo, core).
Axes of the slice: x: 4, y: 8 (y_hi: 4, y_lo: 2; y = y_hi * 2 + y_lo), z: 8, core: 2. Of those that a mesh axis runs over, the one named last changes fastest.
Arguments:
- master: float32 [4, 512, 8192], P('grp', 'dp'), may hold values from -6 to 6
- first_moment: float32 [4, 512, 8192], P('grp', 'dp'), may hold values from -0.03 to 0.03
- second_moment: float32 [4, 512, 8192], P('grp', 'dp'), may hold values from 1e-05 to 0.01
- gradient: bfloat16 [4, 512, 8192], P('grp', 'dp'), may hold values from -0.29882812 to 0.29882812
- checkpoints: float32 [3, 4, 128, 2, 12, 2048], P(None, 'grp', 'dp'), as said below
- block_holder: int32 [4, 128, 16], P('grp', 'dp'), may hold values from 1 to 2, as said below
- failed_member: int32 [128], P('dp'), may hold values from 0 to 3
Outputs:
- new_master: float32 [4, 512, 8192], P('grp', 'dp')
- new_first: float32 [4, 512, 8192], P('grp', 'dp')
- new_second: float32 [4, 512, 8192], P('grp', 'dp')
- weights: bfloat16 [4, 512, 8192], P('grp')
Inputs may be any that keep to these rules, and one draw needn't show every extreme that they name: `block_holder`: each value is 1 or 2. For every shard, at most 12 blocks carry each value, and at each dp index some shard has exactly 12 blocks with value 1. The checkpoint slots of a holder for a source are filled in increasing block order; slots past the count hold stale data. `checkpoints`: row 0 holds master values, row 1 first moments, row 2 second moments, positive.
All inputs are finite; a program needn't handle non-finite values.
Results may differ from a plain program's by a relative error of at most 0.005.
Values may be sent and summed in bfloat16 or wider, within the bound.
A program may use at most 64 MiB of HBM per device.

v0:
```python
import jax
import jax.numpy as jnp
from jax import lax
from jax.sharding import PartitionSpec as P

beta_one = 0.9
beta_two = 0.95
learning_rate = 0.05
weight_decay = 0.1
epsilon = 1e-08
correct_one = 1.0 - 0.9**10
correct_two = 1.0 - 0.95**10


def passed_along(value, axis, steps):
    count = lax.axis_size(axis)
    pairs = [(source, (source + steps) % count) for source in range(count)]
    return lax.ppermute(value, axis, pairs)


def adamw_step(master, first, second, gradient):
    grad_float = gradient.astype(jnp.float32)
    new_first = beta_one * first + (1.0 - beta_one) * grad_float
    new_second = beta_two * second + (1.0 - beta_two) * grad_float * grad_float
    update = new_first / correct_one / (jnp.sqrt(new_second / correct_two) + epsilon)
    new_master = master - learning_rate * (update + weight_decay * master)
    return (new_master, new_first, new_second)


def select_blocks(buffer, holder_ids, offset):
    is_held = holder_ids == offset
    slot_index = jnp.cumsum(is_held.astype(jnp.int32)) - 1
    slot_ids = jnp.arange(buffer.shape[1], dtype=jnp.int32)
    lookup = (is_held[:, None] & (slot_index[:, None] == slot_ids[None, :])).astype(jnp.float32)
    return jnp.einsum("bs,ksc->kbc", lookup, buffer, precision=lax.Precision.HIGHEST)


def per_device(
    master, first_moment, second_moment, gradient, checkpoints, block_holder, failed_member
):
    near_buffer = checkpoints[:, 0, 0, 0]
    far_buffer = checkpoints[:, 0, 0, 1]
    near_rows = passed_along(near_buffer.astype(jnp.bfloat16), "grp", -1).astype(near_buffer.dtype)
    far_rows = passed_along(far_buffer, "grp", -2)
    holder_ids = block_holder[0, 0]
    restored = select_blocks(near_rows, holder_ids, 1) + select_blocks(far_rows, holder_ids, 2)
    restored = restored.reshape((3,) + master.shape)
    failed = failed_member[0] == lax.axis_index("grp")
    master_state = jnp.where(failed, restored[0], master)
    first_state = jnp.where(failed, restored[1], first_moment)
    second_state = jnp.where(failed, restored[2], second_moment)
    new_master, new_first, new_second = adamw_step(
        master_state, first_state, second_state, gradient
    )
    weights = lax.all_gather(new_master.astype(jnp.bfloat16), "dp", axis=1, tiled=True)
    return (new_master, new_first, new_second, weights)


def solution(mesh):
    return jax.shard_map(
        per_device,
        mesh=mesh,
        in_specs=(
            P("grp", "dp", None),
            P("grp", "dp", None),
            P("grp", "dp", None),
            P("grp", "dp", None),
            P(None, "grp", "dp", None, None, None),
            P("grp", "dp", None),
            P("dp"),
        ),
        out_specs=(
            P("grp", "dp", None),
            P("grp", "dp", None),
            P("grp", "dp", None),
            P("grp", None, None),
        ),
        check_vma=False,
    )
```

profile of v0, /device:TPU:1, one launch (start us, length us, event | category | flops | bytes accessed | tf_op | source)
XLA Modules:
  0.0 262.9 jit_solution(1890305828507715077)
XLA Ops:
  7.2 0.0 all-gather.2.cloned.1.call-start
  7.2 1.3 slice.29
  8.5 0.1 copy.49
  8.6 8.8 %collective-permute-start = (bf16[3,12,2048]{2,1,0:T(8,128)(2,1)S(1)}, bf16[3,12,2048]{2,1,0:T(8,128)(2,1)S(1)}, u32[]{:S(2)}, u32[]{:S(2)}) collective-permute-start(bf16[3,12,2048]{2,1,0:T(8,128)(2,1)S(1)} %bitcast.27), channel_id=1, source_target_pairs={{0,3},{1,0},{2,1},{3,2},{4,7},{5,4},{6,5},{7,6},{8,11},{9,8},{10,9... | collective-permute-start | bytes 442376 | tf_op jit(solution)/shard_map/ppermute | solution.py:18
  17.4 1.4 slice.20
  18.8 0.1 copy.48
  18.9 1.9 collective-permute-start.1
  20.8 0.7 compare_bitcast_fusion.1
  22.1 0.1 copy.39
  22.2 0.1 copy.40
  22.3 0.1 add_reduce_fusion.1
  22.5 0.1 add_reduce_fusion
  22.6 8.9 %collective-permute-done.1 = f32[3,12,2048]{2,1,0:T(8,128)S(1)} collective-permute-done((f32[3,12,2048]{2,1,0:T(8,128)S(1)}, f32[3,12,2048]{2,1,0:T(8,128)S(1)}, u32[]{:S(2)}, u32[]{:S(2)}) %collective-permute-start.1) | collective-permute-done | bytes 294944 | tf_op jit(solution)/shard_map/ppermute | solution.py:18
  31.5 0.4 fusion.8
  31.9 0.0 collective-permute-done
  31.9 0.3 fusion
  32.2 0.1 squeeze.21
  32.3 0.1 squeeze.20
  32.3 0.1 squeeze.19
  32.4 2.0 fusion.16
  34.5 0.8 copy.42
  35.2 0.0 all-gather.2.cloned.1.call-update
  35.3 204.2 %all-gather.2.cloned.1.call-done = bf16[1,512,8192]{2,0,1:T(2,128)(2,1)} async-done(((bf16[1,4,8192]{2,0,1:T(2,128)(2,1)}), bf16[1,512,8192]{2,0,1:T(2,128)(2,1)}) %all-gather.2.cloned.1.call-update) | async-done | bytes 8388624 | tf_op jit(solution)/shard_map/all_gather | solution.py:55
  239.4 16.6 %copy.43 = bf16[1,512,8192]{2,1,0:T(8,128)(2,1)} copy(bf16[1,512,8192]{2,0,1:T(2,128)(2,1)} %all-gather.2.cloned.1.call-done) | data formatting | bytes 16777216
  (3 shorter events, 0.1 us)
Async XLA Ops:
  7.2 232.3 %all-gather.2.cloned.1.call-start = ((), (), s32[]{:S(2)}) async-start(), calls=%async_computation | async-start | bytes 16908288 | tf_op jit(solution)/shard_map/all_gather | solution.py:55
  8.6 23.3 %collective-permute-start = (bf16[3,12,2048]{2,1,0:T(8,128)(2,1)S(1)}, bf16[3,12,2048]{2,1,0:T(8,128)(2,1)S(1)}, u32[]{:S(2)}, u32[]{:S(2)}) collective-permute-start(bf16[3,12,2048]{2,1,0:T(8,128)(2,1)S(1)} %bitcast.27), channel_id=1, source_target_pairs={{0,3},{1,0},{2,1},{3,2},{4,7},{5,4},{6,5},{7,6},{8,11},{9,8},{10,9... | collective-permute-start | bytes 442376 | tf_op jit(solution)/shard_map/ppermute | solution.py:18
  18.9 12.6 %collective-permute-start.1 = (f32[3,12,2048]{2,1,0:T(8,128)S(1)}, f32[3,12,2048]{2,1,0:T(8,128)S(1)}, u32[]{:S(2)}, u32[]{:S(2)}) collective-permute-start(f32[3,12,2048]{2,1,0:T(8,128)S(1)} %bitcast.26), channel_id=1, source_target_pairs={{0,2},{1,3},{2,0},{3,1},{4,6},{5,7},{6,4},{7,5},{8,10},{9,11},{10,... | collective-permute-start | bytes 884744 | tf_op jit(solution)/shard_map/ppermute | solution.py:18
Sparse Core Ops, SparseCore 0:
  35.4 204.0 all-gather.1
where the time goes:
time: 263 us
  waiting for transfers between devices  213 us (81%)
  local copies, waits for them, and re-layouts  20.6 us (8%)
  between operations  14.8 us (6%)
  starting transfers between devices  10.7 us (4%)
  other arithmetic  2.99 us (1%)
    all_gather x1, waiting for transfers between devices, per_device(): lax.all_gather(new_master.astype(jnp.bfloat16), 'dp', axis=1, tiled=True)  204 us
    unnamed x3, local copies, waits for them, and re-layouts  16.8 us
    ppermute x2, starting transfers between devices, passed_along(): return lax.ppermute(value, axis, pairs)  10.7 us
    ppermute x2, waiting for transfers between devices, passed_along(): return lax.ppermute(value, axis, pairs)  8.92 us
  transfers between devices with their start and end apart: 3, of which 2 were waited for; matrix products, arithmetic and copies ran while one was open for 1% of the time, Pallas kernels for 0%

commit v1 on v0

v1 whole, which is shorter than its diff:
```python
import functools

import jax
import jax.numpy as jnp
from jax import lax
from jax.experimental import pallas as pl
from jax.experimental.pallas import tpu as pltpu
from jax.sharding import PartitionSpec as P

MESH = pl.DeviceIdType.MESH
NX, NZ, NY = 4, 8, 4
STEPS = ((1, 0, 0), (-1, 0, 0), (0, 1, 0), (0, -1, 0), (0, 0, 1), (0, 0, -1))

TREE = (
    (0, 2, 3, 4, 5, 1, 0), (4, 0, 2, 1), (28, 3, 4, 0, 5), (96, 3, 1), (32,), (1, 2, 1, 4, 0), (3, 0, 1, 2),
    (36, 2), (8, 5, 2, 1), (100, 1), (24, 3, 5), (60, 3, 4), (5, 2, 1, 0), (64,), (124, 1, 3), (29, 3, 4),
    (31,), (33, 0), (7, 0, 1), (97, 3), (20, 0, 5, 1), (35, 5, 0, 3), (40, 2), (99, 3), (2, 2, 1), (11, 5, 2,
    0, 1), (56, 0, 4), (37,), (12, 2, 1), (104,), (120,), (65,), (9, 1, 2, 0), (68, 2), (61,), (27, 0, 5),
    (25, 3), (39,), (44, 4, 0, 5), (101, 1), (125, 1, 3), (52, 4, 3), (6, 0), (92,), (30, 0), (23, 3), (63,),
    (67, 2), (15, 1), (103,), (127, 3, 5, 1), (43,), (16,), (116, 3), (57,), (34, 0), (21, 4, 1), (88, 3, 5),
    (13, 2), (98, 2), (121,), (41,), (72, 5), (107,), (45, 4), (10, 2, 1, 0), (48,), (59, 3), (71,), (108,),
    (19, 1), (76, 5), (17,), (105, 2), (53, 3, 4), (26, 0), (123, 3), (38,), (69, 2), (102,), (112, 1), (62,
    0), (14, 2), (93, 3), (22, 1), (47,), (84,), (66, 2), (109, 2), (111,), (55, 3, 0), (42,), (73, 4, 2),
    (95,), (46, 0), (126, 3), (49, 0), (58,), (18, 0), (117,), (119,), (94, 3), (70,), (106, 2), (54, 0),
    (91,), (89, 3), (87,), (113, 4), (115, 1), (51,), (78, 2), (77,), (80,), (74,), (75,), (122,), (81,),
    (110,), (118,), (90,), (50,), (83,), (82,), (79,), (114,), (85,), (86,),
)

beta_one = 0.9
beta_two = 0.95
learning_rate = 0.05
weight_decay = 0.1
epsilon = 1e-08
correct_one = 1.0 - 0.9**10
correct_two = 1.0 - 0.95**10


def moved(cell, direction):
    x, z, y = cell // 32, cell // 4 % 8, cell % 4
    a, b, c = STEPS[direction]
    return ((x + a) % NX * 8 + (z + b) % NZ) * 4 + (y + c) % NY


def fold(rows):
    return jnp.concatenate([rows[:, 2048 * q : 2048 * q + 2048] for q in range(4)], axis=0)


def unfold(folded):
    return jnp.concatenate([folded[4 * q : 4 * q + 4] for q in range(4)], axis=1)


def adamw_step(master, first, second, grad_float):
    new_first = beta_one * first + (1.0 - beta_one) * grad_float
    new_second = beta_two * second + (1.0 - beta_two) * grad_float * grad_float
    update = new_first / correct_one / (jnp.sqrt(new_second / correct_two) + epsilon)
    new_master = master - learning_rate * (update + weight_decay * master)
    return (new_master, new_first, new_second)


def gather_kernel(
    holder_ref, failed_ref, ckpt_hbm, master_hbm, first_hbm, second_hbm, grad_hbm,
    gathered, master_out, first_out, second_out,
    ckpt, state, grad, send_a, send_b, recv_a, recv_b,
    load_sem, ex_send, ex_recv, ag_send, ag_recv,
):
    dp = lax.axis_index("dp")
    grp = lax.axis_index("grp")
    x, z, y = dp // 32, lax.rem(dp // 4, 8), lax.rem(dp, 4)

    def slot(dx, dz, dy):
        return (lax.rem(x + dx + NX, NX) * 8 + lax.rem(z + dz + NZ, NZ)) * 4 + lax.rem(y + dy + NY, NY)

    neighbours = [(slot(*step), grp) for step in STEPS]
    peers = [(dp, lax.rem(grp + k, 4)) for k in (1, 2, 3)]

    loads = [pltpu.make_async_copy(ckpt_hbm, ckpt, load_sem.at[0])]
    for i, ref in enumerate((master_hbm, first_hbm, second_hbm)):
        loads.append(pltpu.make_async_copy(ref, state.at[i], load_sem.at[i + 1]))
    loads.append(pltpu.make_async_copy(grad_hbm, grad, load_sem.at[4]))
    for load in loads:
        load.start()

    barrier = pltpu.get_barrier_semaphore()
    for device in neighbours + peers:
        pl.semaphore_signal(barrier, inc=1, device_id=device, device_id_type=MESH)

    loads[0].wait()
    for o in range(2):
        for k in range(3):
            head = ckpt[k, o, 0:8, :]
            tail = ckpt[k, o, 8:12, :]
            send_a[o, k] = jnp.concatenate([head[:, :1024], head[:, 1024:]], axis=0).astype(jnp.bfloat16)
            send_b[o, k] = jnp.concatenate(
                [tail[:, 512 * c : 512 * c + 512] for c in range(4)], axis=0
            ).astype(jnp.bfloat16)
    pl.semaphore_wait(barrier, len(neighbours) + len(peers))

    exchange = []
    for part, (src, dst) in enumerate(((send_a, recv_a), (send_b, recv_b))):
        for o in (1, 0):
            copy = pltpu.make_async_remote_copy(
                src_ref=src.at[o],
                dst_ref=dst.at[o],
                send_sem=ex_send.at[2 * part + o],
                recv_sem=ex_recv.at[2 * part + o],
                device_id=peers[2 - o],
                device_id_type=MESH,
            )
            copy.start()
            exchange.append(copy)

    rows = lax.broadcasted_iota(jnp.int32, (16, 32), 0)
    wanted = jnp.zeros((16, 32), jnp.int32)
    seen_near = jnp.int32(0)
    for b in range(16):
        near = holder_ref[0, b] == 1
        s = jnp.where(near, seen_near, b - seen_near)
        source = s + jnp.where(near, jnp.where(s < 8, 0, 8), jnp.where(s < 8, 8, 12))
        wanted = jnp.where(rows == 4 * (b % 4) + b // 4, source, wanted)
        seen_near = seen_near + jnp.where(near, 1, 0)
    lookup = jnp.where(lax.broadcasted_iota(jnp.int32, (16, 32), 1) == wanted, 1.0, 0.0).astype(jnp.bfloat16)
    failed = failed_ref[0] == grp

    for load in loads[1:]:
        load.wait()
    local = [fold(state[k]) for k in range(3)]
    grad_float = fold(grad[...].astype(jnp.float32))
    for copy in exchange:
        copy.wait_recv()
    chosen = []
    for k in range(3):
        parts = []
        for o in range(2):
            a = recv_a[o, k].astype(jnp.float32)
            parts.append(jnp.concatenate([a[:8], a[8:]], axis=1))
        tails = []
        for o in range(2):
            b = recv_b[o, k].astype(jnp.float32)
            tails.append(jnp.concatenate([b[4 * c : 4 * c + 4] for c in range(4)], axis=1))
        parts.append(jnp.concatenate(tails, axis=0))
        parts.append(jnp.zeros((8, 2048), jnp.float32))
        held = jnp.concatenate(parts, axis=0).astype(jnp.bfloat16)
        restored = jnp.dot(lookup, held, preferred_element_type=jnp.float32)
        chosen.append(jnp.where(failed, restored, local[k]))
    new_master, new_first, new_second = adamw_step(*chosen, grad_float)
    gathered[dp] = new_master.astype(jnp.bfloat16)

    def copy_of(cell, direction):
        there = moved(cell, direction)
        place = gathered.at[slot(-(cell // 32), -(cell // 4 % 8), -(cell % 4))]
        return pltpu.make_async_remote_copy(
            src_ref=place,
            dst_ref=place,
            send_sem=ag_send.at[there],
            recv_sem=ag_recv.at[there],
            device_id=neighbours[direction],
            device_id_type=MESH,
        )

    def arrival_of(cell):
        place = gathered.at[slot(-(cell // 32), -(cell // 4 % 8), -(cell % 4))]
        return pltpu.make_async_remote_copy(
            src_ref=place,
            dst_ref=place,
            send_sem=ag_send.at[cell],
            recv_sem=ag_recv.at[cell],
            device_id=neighbours[0],
            device_id_type=MESH,
        )

    sent = []
    for cell, *directions in TREE:
        if cell:
            arrival_of(cell).wait_recv()
        for direction in directions:
            copy = copy_of(cell, direction)
            copy.start()
            sent.append(copy)
        if not cell:
            master_out[...] = unfold(new_master)
            first_out[...] = unfold(new_first)
            second_out[...] = unfold(new_second)
            for copy in exchange:
                copy.wait_send()
    for copy in sent:
        copy.wait_send()


def place_kernel(gathered, master, first, second, weights, master_out, first_out, second_out, sem):
    step = pl.program_id(0)
    copies = [
        pltpu.make_async_copy(src, dst, sem.at[i])
        for i, (src, dst) in enumerate(((master, master_out), (first, first_out), (second, second_out)))
    ]

    @pl.when(step == 0)
    def _():
        for copy in copies:
            copy.start()

    for t in range(2):
        shards = [gathered[(2 * step + t) * 4 + k].astype(jnp.float32) for k in range(4)]
        for q in range(4):
            tile = jnp.concatenate([shard[4 * q : 4 * q + 4] for shard in shards], axis=0)
            weights[16 * t : 16 * t + 16, 2048 * q : 2048 * q + 2048] = tile.astype(jnp.bfloat16)

    @pl.when(step == pl.num_programs(0) - 1)
    def _():
        for copy in copies:
            copy.wait()


def per_device(master, first_moment, second_moment, gradient, checkpoints, block_holder, failed_member):
    rows = jax.ShapeDtypeStruct((4, 8192), jnp.float32)
    gathered, new_master, new_first, new_second = pl.pallas_call(
        gather_kernel,
        out_shape=[pltpu.VMEM((128, 16, 2048), jnp.bfloat16)] + [pltpu.VMEM((4, 8192), jnp.float32)] * 3,
        in_specs=[pl.BlockSpec(memory_space=pltpu.SMEM)] * 2 + [pl.BlockSpec(memory_space=pl.ANY)] * 5,
        out_specs=[pl.BlockSpec(memory_space=pltpu.VMEM)] * 4,
        scratch_shapes=[
            pltpu.VMEM((3, 2, 12, 2048), jnp.float32),
            pltpu.VMEM((3, 4, 8192), jnp.float32),
            pltpu.VMEM((4, 8192), jnp.bfloat16),
            pltpu.VMEM((2, 3, 16, 1024), jnp.bfloat16),
            pltpu.VMEM((2, 3, 16, 512), jnp.bfloat16),
            pltpu.VMEM((2, 3, 16, 1024), jnp.bfloat16),
            pltpu.VMEM((2, 3, 16, 512), jnp.bfloat16),
            pltpu.SemaphoreType.DMA((5,)),
            pltpu.SemaphoreType.DMA((4,)),
            pltpu.SemaphoreType.DMA((4,)),
            pltpu.SemaphoreType.DMA((128,)),
            pltpu.SemaphoreType.DMA((128,)),
        ],
        compiler_params=pltpu.CompilerParams(
            collective_id=0, has_side_effects=True, vmem_limit_bytes=40 * 2**20
        ),
        name="restore_step_gather",
    )(
        block_holder.reshape(1, 16), failed_member, checkpoints.reshape(3, 2, 12, 2048), master.reshape(4, 8192),
        first_moment.reshape(4, 8192), second_moment.reshape(4, 8192), gradient.reshape(4, 8192),
    )
    weights, new_master, new_first, new_second = pl.pallas_call(
        place_kernel,
        grid=(16,),
        out_shape=[jax.ShapeDtypeStruct((512, 8192), jnp.bfloat16), rows, rows, rows],
        in_specs=[pl.BlockSpec(memory_space=pltpu.VMEM)] * 4,
        out_specs=[pl.BlockSpec((16 * 2, 8192), lambda i: (i, 0))] + [pl.BlockSpec(memory_space=pl.ANY)] * 3,
        scratch_shapes=[pltpu.SemaphoreType.DMA((3,))],
        compiler_params=pltpu.CompilerParams(vmem_limit_bytes=40 * 2**20),
        name="place_rows",
    )(gathered, new_master, new_first, new_second)
    whole = (1, 4, 8192)
    return (
        new_master.reshape(whole), new_first.reshape(whole), new_second.reshape(whole), weights.reshape(1, 512, 8192)
    )


def solution(mesh):
    return jax.shard_map(
        per_device,
        mesh=mesh,
        in_specs=(
            P("grp", "dp", None),
            P("grp", "dp", None),
            P("grp", "dp", None),
            P("grp", "dp", None),
            P(None, "grp", "dp", None, None, None),
            P("grp", "dp", None),
            P("dp"),
        ),
        out_specs=(
            P("grp", "dp", None),
            P("grp", "dp", None),
            P("grp", "dp", None),
            P("grp", None, None),
        ),
        check_vma=False,
    )
```

time: 263 us -> 80.4 us (0.31)
  the two profiles are of different devices: /device:TPU:1 before, /device:TPU:8 now
where the time goes in v1:
time: 80.4 us; the launch traced here: 80.1 us
  Pallas kernels  73.2 us (91%)
  local copies, waits for them, and re-layouts  5.62 us (7%)
  between operations  1.3 us (2%)
    pallas_call x1, Pallas kernels, per_device(): pl.pallas_call(gather_kernel, out_shape=[pltpu.VMEM((128, 16, 2048), jnp....  65.4 us
    pallas_call x1, Pallas kernels, per_device(): pl.pallas_call(place_kernel, grid=(16,), out_shape=[jax.ShapeDtypeStruct(...  7.72 us
    unnamed x11, local copies, waits for them, and re-layouts  5.62 us

profile of v1, /device:TPU:8, one launch (start us, length us, event | category | flops | bytes accessed | tf_op | source)
XLA Modules:
  0.0 80.1 jit_solution(11537203533914280279)
XLA Ops:
  1.3 1.4 %copy.13 = f32[3,1,1,2,12,2048]{5,4,3,0,2,1:T(8,128)S(1)} copy(f32[3,1,1,2,12,2048]{5,3,4,2,1,0:T(2,128)} %param.11) | data formatting | bytes 1179648 | tf_op args[4]
  2.7 0.0 copy-start
  2.7 0.9 %copy-done = f32[1,4,8192]{2,1,0:T(4,128)S(1)} copy-done((f32[1,4,8192]{2,1,0:T(4,128)S(1)}, f32[1,4,8192]{2,1,0:T(4,128)}, u32[]{:S(2)}) %copy-start) | copy-done | bytes 131096
  3.6 0.0 copy-start.1
  3.6 0.9 %copy-done.1 = f32[1,4,8192]{2,1,0:T(4,128)S(1)} copy-done((f32[1,4,8192]{2,1,0:T(4,128)S(1)}, f32[1,4,8192]{2,1,0:T(4,128)}, u32[]{:S(2)}) %copy-start.1) | copy-done | bytes 131096
  4.5 0.0 copy-start.2
  4.5 0.9 %copy-done.2 = f32[1,4,8192]{2,1,0:T(4,128)S(1)} copy-done((f32[1,4,8192]{2,1,0:T(4,128)S(1)}, f32[1,4,8192]{2,1,0:T(4,128)}, u32[]{:S(2)}) %copy-start.2) | copy-done | bytes 131096
  5.4 0.0 copy-start.3
  5.4 0.8 %copy-done.3 = bf16[1,4,8192]{2,1,0:T(4,128)(2,1)S(1)} copy-done((bf16[1,4,8192]{2,1,0:T(4,128)(2,1)S(1)}, bf16[1,4,8192]{2,1,0:T(4,128)(2,1)}, u32[]{:S(2)}) %copy-start.3) | copy-done | bytes 65560
  6.3 0.0 copy-start.4
  6.3 0.7 copy-done.4
  6.9 65.4 %restore_step_gather.1 = (bf16[128,16,2048]{2,1,0:T(8,128)(2,1)S(1)}, f32[4,8192]{1,0:T(4,128)S(1)}, f32[4,8192]{1,0:T(4,128)S(1)}, f32[4,8192]{1,0:T(4,128)S(1)}) custom-call(s32[1,16]{1,0:T(1,128)S(1)} %bitcast.17, s32[1]{0:T(128)S(6)} %copy.14.failed_ref, f32[3,2,12,2048]{3,2,1,0:T(8,128)S(1)} %bitcast.12, f32[4,8192]{1,0:T(4,128)S(1)} %bitcast.13, ...), custom_call_target="tpu_custom_call" | custom-call | tf_op jit(solution)/shard_map/restore_step_gather/pallas_call | solution.py:215
  72.4 7.7 %place_rows.1 = (bf16[512,8192]{1,0:T(8,128)(2,1)}, f32[4,8192]{1,0:T(4,128)}, f32[4,8192]{1,0:T(4,128)}, f32[4,8192]{1,0:T(4,128)}) custom-call(bf16[128,16,2048]{2,1,0:T(8,128)(2,1)S(1)} %get-tuple-element.12.gathered, f32[4,8192]{1,0:T(4,128)S(1)} %get-tuple-element.13.master, f32[4,8192]{1,0:T(4,128)S(1)} %get-tuple-element.14.first, ...), custom_call_target="tpu_custom_call" | custom-call | tf_op jit(solution)/shard_map/place_rows/pallas_call | solution.py:242
Async XLA Ops:
  2.7 0.9 %copy-start = (f32[1,4,8192]{2,1,0:T(4,128)S(1)}, f32[1,4,8192]{2,1,0:T(4,128)}, u32[]{:S(2)}) copy-start(f32[1,4,8192]{2,1,0:T(4,128)} %param.7) | copy-start | bytes 393220
  3.6 0.9 %copy-start.1 = (f32[1,4,8192]{2,1,0:T(4,128)S(1)}, f32[1,4,8192]{2,1,0:T(4,128)}, u32[]{:S(2)}) copy-start(f32[1,4,8192]{2,1,0:T(4,128)} %param.8) | copy-start | bytes 393220
  4.5 0.9 %copy-start.2 = (f32[1,4,8192]{2,1,0:T(4,128)S(1)}, f32[1,4,8192]{2,1,0:T(4,128)}, u32[]{:S(2)}) copy-start(f32[1,4,8192]{2,1,0:T(4,128)} %param.9) | copy-start | bytes 393220
  5.4 0.8 %copy-start.3 = (bf16[1,4,8192]{2,1,0:T(4,128)(2,1)S(1)}, bf16[1,4,8192]{2,1,0:T(4,128)(2,1)}, u32[]{:S(2)}) copy-start(bf16[1,4,8192]{2,1,0:T(4,128)(2,1)} %param.10) | copy-start | bytes 196612
  6.3 0.7 copy-start.4

commit v2 on v1

v2 whole, which is shorter than its diff:
```python
import functools

import jax
import jax.numpy as jnp
from jax import lax
from jax.experimental import pallas as pl
from jax.experimental.pallas import tpu as pltpu
from jax.sharding import PartitionSpec as P

MESH = pl.DeviceIdType.MESH
NX, NZ, NY = 4, 8, 4
STEPS = ((1, 0, 0), (-1, 0, 0), (0, 1, 0), (0, -1, 0), (0, 0, 1), (0, 0, -1))

TREE = (
    (0, 2, 3, 4, 5, 1, 0), (4, 0, 2, 1), (28, 3, 4, 0, 5), (96, 3, 1), (32,), (1, 2, 1, 4, 0), (3, 0, 1, 2),
    (36, 2), (8, 5, 2, 1), (100, 1), (24, 3, 5), (60, 3, 4), (5, 2, 1, 0), (64,), (124, 1, 3), (29, 3, 4),
    (31,), (33, 0), (7, 0, 1), (97, 3), (20, 0, 5, 1), (35, 5, 0, 3), (40, 2), (99, 3), (2, 2, 1), (11, 5, 2,
    0, 1), (56, 0, 4), (37,), (12, 2, 1), (104,), (120,), (65,), (9, 1, 2, 0), (68, 2), (61,), (27, 0, 5),
    (25, 3), (39,), (44, 4, 0, 5), (101, 1), (125, 1, 3), (52, 4, 3), (6, 0), (92,), (30, 0), (23, 3), (63,),
    (67, 2), (15, 1), (103,), (127, 3, 5, 1), (43,), (16,), (116, 3), (57,), (34, 0), (21, 4, 1), (88, 3, 5),
    (13, 2), (98, 2), (121,), (41,), (72, 5), (107,), (45, 4), (10, 2, 1, 0), (48,), (59, 3), (71,), (108,),
    (19, 1), (76, 5), (17,), (105, 2), (53, 3, 4), (26, 0), (123, 3), (38,), (69, 2), (102,), (112, 1), (62,
    0), (14, 2), (93, 3), (22, 1), (47,), (84,), (66, 2), (109, 2), (111,), (55, 3, 0), (42,), (73, 4, 2),
    (95,), (46, 0), (126, 3), (49, 0), (58,), (18, 0), (117,), (119,), (94, 3), (70,), (106, 2), (54, 0),
    (91,), (89, 3), (87,), (113, 4), (115, 1), (51,), (78, 2), (77,), (80,), (74,), (75,), (122,), (81,),
    (110,), (118,), (90,), (50,), (83,), (82,), (79,), (114,), (85,), (86,),
)

beta_one = 0.9
beta_two = 0.95
learning_rate = 0.05
weight_decay = 0.1
epsilon = 1e-08
correct_one = 1.0 - 0.9**10
correct_two = 1.0 - 0.95**10


def moved(cell, direction):
    x, z, y = cell // 32, cell // 4 % 8, cell % 4
    a, b, c = STEPS[direction]
    return ((x + a) % NX * 8 + (z + b) % NZ) * 4 + (y + c) % NY


def adamw_step(master, first, second, grad_float):
    new_first = beta_one * first + (1.0 - beta_one) * grad_float
    new_second = beta_two * second + (1.0 - beta_two) * grad_float * grad_float
    update = new_first / correct_one / (jnp.sqrt(new_second / correct_two) + epsilon)
    new_master = master - learning_rate * (update + weight_decay * master)
    return (new_master, new_first, new_second)


def gather_kernel(
    failed_at, holder_hbm, ckpt_hbm, master_hbm, first_hbm, second_hbm, grad_hbm,
    weights, master_out, first_out, second_out,
    gathered, ckpt, state, grad, restored, send, recv, holder,
    load_sem, ex_send, ex_recv, ag_send, ag_recv,
):
    dp = lax.axis_index("dp")
    grp = lax.axis_index("grp")
    x, z, y = dp // 32, lax.rem(dp // 4, 8), lax.rem(dp, 4)

    def line(dx, dz):
        return lax.rem(x + dx + NX, NX) * 8 + lax.rem(z + dz + NZ, NZ)

    def slot(dx, dz, dy):
        return line(dx, dz) * 4 + lax.rem(y + dy + NY, NY)

    neighbours = [(slot(*step), grp) for step in STEPS]
    peers = [(dp, lax.rem(grp + k, 4)) for k in (1, 2, 3)]

    loads = [
        pltpu.make_async_copy(src, dst, load_sem.at[i])
        for i, (src, dst) in enumerate(
            (
                (ckpt_hbm, ckpt), (master_hbm, state.at[0]), (first_hbm, state.at[1]), (second_hbm, state.at[2]),
                (grad_hbm, grad), (holder_hbm, holder),
            )
        )
    ]
    for load in loads:
        load.start()

    barrier = pltpu.get_barrier_semaphore()
    for device in neighbours + peers:
        pl.semaphore_signal(barrier, inc=1, device_id=device, device_id_type=MESH)

    loads[0].wait()
    for s in range(12):
        for k in range(3):
            for o in range(2):
                send[o, s, k] = ckpt[k, s, pl.ds(o, 16, stride=2), :].astype(jnp.bfloat16)
    pl.semaphore_wait(barrier, len(neighbours) + len(peers))

    exchange = []
    for part in range(1):
        slots = pl.ds(part * 12, 12)
        for o in (1, 0):
            copy = pltpu.make_async_remote_copy(
                src_ref=send.at[o, slots],
                dst_ref=recv.at[o, slots],
                send_sem=ex_send.at[2 * part + o],
                recv_sem=ex_recv.at[2 * part + o],
                device_id=peers[2 - o],
                device_id_type=MESH,
            )
            copy.start()
            exchange.append(copy)
    for load in loads[1:]:
        load.wait()

    places = []
    seen_near = jnp.int32(0)
    for b in range(16):
        near = holder[0, b] == 1
        places.append((jnp.where(near, 0, 1), jnp.minimum(jnp.where(near, seen_near, b - seen_near), 11)))
        seen_near = seen_near + jnp.where(near, 1, 0)
    failed = failed_at[0] == grp
    for copy in exchange:
        copy.wait_recv()
    for b, (o, s) in enumerate(places):
        for k in range(3):
            restored[k, pl.ds(64 * (b % 4) + b // 4, 16, stride=4), :] = recv[o, s, k].astype(jnp.float32)
    chosen = [jnp.where(failed, restored[k], state[k]) for k in range(3)]
    new_master, new_first, new_second = adamw_step(*chosen, grad[...].astype(jnp.float32))
    gathered[dp] = new_master.astype(jnp.bfloat16)

    def copy_of(cell, direction):
        there = moved(cell, direction)
        place = gathered.at[slot(-(cell // 32), -(cell // 4 % 8), -(cell % 4))]
        return pltpu.make_async_remote_copy(
            src_ref=place,
            dst_ref=place,
            send_sem=ag_send.at[there],
            recv_sem=ag_recv.at[there],
            device_id=neighbours[direction],
            device_id_type=MESH,
        )

    def arrival_of(cell):
        place = gathered.at[slot(-(cell // 32), -(cell // 4 % 8), -(cell % 4))]
        return pltpu.make_async_remote_copy(
            src_ref=place,
            dst_ref=place,
            send_sem=ag_send.at[cell],
            recv_sem=ag_recv.at[cell],
            device_id=neighbours[0],
            device_id_type=MESH,
        )

    def place_rows(dx, dz):
        t = line(-dx, -dz)

        def columns(j, carry):
            for i in range(4):
                at = pl.multiple_of((4 * j + i) * 16, 16)
                shards = [gathered[4 * t + k, pl.ds(at, 16), :].astype(jnp.float32) for k in range(4)]
                for c in range(4):
                    tile = jnp.concatenate([shard[4 * c : 4 * c + 4] for shard in shards], axis=0)
                    lanes = pl.multiple_of((4 * j + i) * 512 + 128 * c, 128)
                    weights[pl.ds(pl.multiple_of(16 * t, 16), 16), pl.ds(lanes, 128)] = tile.astype(jnp.bfloat16)
            return carry

        lax.fori_loop(0, 16 // 4, columns, 0)

    sent = []
    arrived = [0] * 32
    ready = []
    for cell, *directions in TREE:
        if cell:
            arrival_of(cell).wait_recv()
        for direction in directions:
            copy = copy_of(cell, direction)
            copy.start()
            sent.append(copy)
        if not cell:
            master_out[...] = new_master
            first_out[...] = new_first
            second_out[...] = new_second
            for copy in exchange:
                copy.wait_send()
        arrived[cell // 4] += 1
        if arrived[cell // 4] == 4:
            ready.append(cell // 4)
        if ready:
            done = ready.pop(0)
            place_rows(done // 8, done % 8)
    for done in ready:
        place_rows(done // 8, done % 8)
    for copy in sent:
        copy.wait_send()


def output_kernel(*refs):
    copies = [pltpu.make_async_copy(refs[i], refs[i + 4], refs[8].at[i]) for i in range(3)]
    for i in range(8):
        rows = pl.ds(512 // 8 * i, 512 // 8)
        copies.append(pltpu.make_async_copy(refs[3].at[rows], refs[7].at[rows], refs[8].at[3 + i]))
    for copy in copies:
        copy.start()
    for copy in copies:
        copy.wait()


def tiles(rows):
    return rows.reshape(4, 64, 128).transpose(1, 0, 2).reshape(256, 128)


def rows_of(tiled):
    return tiled.reshape(64, 4, 128).transpose(1, 0, 2).reshape(1, 4, 8192)


def per_device(master, first_moment, second_moment, gradient, checkpoints, block_holder, failed_member):
    held = checkpoints.reshape(3, 2, 12, 16, 128).transpose(0, 2, 3, 1, 4).reshape(3, 12, 32, 128)
    operands = [block_holder.reshape(1, 16), held]
    operands += [tiles(value) for value in (master, first_moment, second_moment, gradient)]
    operands = [pltpu.with_memory_space_constraint(value, pltpu.HBM) for value in operands]
    shard = ((256, 128), jnp.float32)
    weights, new_master, new_first, new_second = pl.pallas_call(
        gather_kernel,
        out_shape=[pltpu.VMEM((512, 8192), jnp.bfloat16)] + [pltpu.VMEM(*shard)] * 3,
        in_specs=[pl.BlockSpec(memory_space=pltpu.SMEM)] + [pl.BlockSpec(memory_space=pltpu.HBM)] * 6,
        out_specs=[pl.BlockSpec(memory_space=pltpu.VMEM)] * 4,
        scratch_shapes=[
            pltpu.VMEM((128, 256, 128), jnp.bfloat16),
            pltpu.VMEM((3, 12, 32, 128), jnp.float32),
            pltpu.VMEM((3, 256, 128), jnp.float32),
            pltpu.VMEM((256, 128), jnp.bfloat16),
            pltpu.VMEM((3, 256, 128), jnp.float32),
            pltpu.VMEM((2, 12, 3, 16, 128), jnp.bfloat16),
            pltpu.VMEM((2, 12, 3, 16, 128), jnp.bfloat16),
            pltpu.SMEM((1, 16), jnp.int32),
            pltpu.SemaphoreType.DMA((6,)),
            pltpu.SemaphoreType.DMA((2 * 1,)),
            pltpu.SemaphoreType.DMA((2 * 1,)),
            pltpu.SemaphoreType.DMA((128,)),
            pltpu.SemaphoreType.DMA((128,)),
        ],
        compiler_params=pltpu.CompilerParams(
            collective_id=0, has_side_effects=True, vmem_limit_bytes=24 * 2**20
        ),
        name="restore_step_gather",
    )(failed_member, *operands)
    results = [
        pltpu.with_memory_space_constraint(value, pltpu.VMEM) for value in (new_master, new_first, new_second, weights)
    ]
    new_master, new_first, new_second, weights = pl.pallas_call(
        output_kernel,
        out_shape=[jax.ShapeDtypeStruct(*shard)] * 3 + [jax.ShapeDtypeStruct((512, 8192), jnp.bfloat16)],
        in_specs=[pl.BlockSpec(memory_space=pltpu.VMEM)] * 4,
        out_specs=[pl.BlockSpec(memory_space=pl.ANY)] * 4,
        scratch_shapes=[pltpu.SemaphoreType.DMA((3 + 8,))],
        compiler_params=pltpu.CompilerParams(vmem_limit_bytes=4 * 2**20),
        name="write_outputs",
    )(*results)
    return (rows_of(new_master), rows_of(new_first), rows_of(new_second), weights.reshape(1, 512, 8192))


def solution(mesh):
    return jax.shard_map(
        per_device,
        mesh=mesh,
        in_specs=(
            P("grp", "dp", None),
            P("grp", "dp", None),
            P("grp", "dp", None),
            P("grp", "dp", None),
            P(None, "grp", "dp", None, None, None),
            P("grp", "dp", None),
            P("dp"),
        ),
        out_specs=(
            P("grp", "dp", None),
            P("grp", "dp", None),
            P("grp", "dp", None),
            P("grp", None, None),
        ),
        check_vma=False,
    )
```

time: 80.4 us -> 71.6 us (0.89)
  the two profiles are of different devices: /device:TPU:8 before, /device:TPU:9 now
where the time goes in v2:
time: 71.6 us; the launch traced here: 71.5 us
  Pallas kernels  70.2 us (98%)
  between operations  1.29 us (2%)
    pallas_call x1, Pallas kernels, per_device(): pl.pallas_call(gather_kernel, out_shape=[pltpu.VMEM((512, 8192), jnp.bflo...  66.7 us
    pallas_call x1, Pallas kernels, per_device(): pl.pallas_call(output_kernel, out_shape=[jax.ShapeDtypeStruct(*shard)] *...  3.52 us

profile of v2, /device:TPU:9, one launch (start us, length us, event | category | flops | bytes accessed | tf_op | source)
XLA Modules:
  0.0 71.5 jit_solution(18070436399918224978)
XLA Ops:
  1.3 66.7 %restore_step_gather.1 = (bf16[512,8192]{1,0:T(8,128)(2,1)S(1)}, f32[256,128]{1,0:T(8,128)S(1)}, f32[256,128]{1,0:T(8,128)S(1)}, f32[256,128]{1,0:T(8,128)S(1)}) custom-call(s32[1]{0:T(128)S(6)} %copy.19.failed_at, s32[1,16]{1,0:T(1,128)} %bitcast.47, f32[3,12,32,128]{3,2,1,0:T(8,128)} %bitcast.42, f32[256,128]{1,0:T(8,128)} %bitcast.43, ...), custom_call_target="tpu_custom_call" | custom-call | tf_op jit(solution)/shard_map/restore_step_gather/pallas_call | solution.py:218
  68.0 3.5 %write_outputs.1 = (f32[256,128]{1,0:T(8,128)}, f32[256,128]{1,0:T(8,128)}, f32[256,128]{1,0:T(8,128)}, bf16[512,8192]{1,0:T(8,128)(2,1)}) custom-call(f32[256,128]{1,0:T(8,128)S(1)} %get-tuple-element.12.refs_0_, f32[256,128]{1,0:T(8,128)S(1)} %get-tuple-element.13.refs_1_, f32[256,128]{1,0:T(8,128)S(1)} %get-tuple-element.14.refs_2_, ...), custom_call_target="tpu_custom_call" | custom-call | tf_op jit(solution)/shard_map/write_outputs/pallas_call | solution.py:246

commit v3 on v2

v3 whole, which is shorter than its diff:
```python
import functools

import jax
import jax.numpy as jnp
from jax import lax
from jax.experimental import pallas as pl
from jax.experimental.pallas import tpu as pltpu
from jax.sharding import PartitionSpec as P

MESH = pl.DeviceIdType.MESH
NX, NZ, NY = 4, 8, 4
PARTS = 3
STEPS = ((1, 0, 0), (-1, 0, 0), (0, 1, 0), (0, -1, 0), (0, 0, 1), (0, 0, -1))

TREE = (
    (0, 0, 5, 4, 3, 2, 1, 0), (0, 28, 3, 0, 1), (0, 4, 2, 1, 0), (0, 96, 1, 5), (0, 32, 4), (0, 3, 2, 5, 3,
    0), (0, 1, 3, 2, 1), (0, 24, 3, 0), (0, 60, 0, 4, 5), (0, 124, 3), (0, 8, 4, 0, 2), (0, 36), (0, 100, 2),
    (0, 7, 1, 2, 0), (0, 31, 1, 3, 5), (0, 99), (0, 33), (0, 35, 0), (0, 64, 2, 4), (0, 5, 0), (0, 29, 1, 3),
    (0, 56, 5), (0, 97, 2), (0, 12, 1), (0, 20, 0, 1, 3), (0, 2, 2, 0, 1), (0, 92, 3), (0, 103, 2, 5), (0,
    61), (0, 104), (0, 120), (0, 40, 2), (0, 127, 1, 3), (0, 11, 2, 0), (0, 27, 3), (0, 39, 0), (0, 125, 4,
    1), (0, 63), (0, 9, 2, 1), (0, 68, 2), (0, 25, 0, 3, 1, 4), (0, 67), (0, 108), (0, 101, 1), (0, 16), (0,
    37, 2), (0, 116, 3, 4), (0, 6, 2, 0), (0, 30), (0, 88), (0, 65), (0, 52, 3, 0), (0, 98), (0, 107, 5), (0,
    123, 1), (0, 34, 3, 0), (0, 95, 5), (0, 44, 4, 0), (0, 23, 3, 1), (0, 59, 3), (0, 126, 3), (0, 43, 2, 0),
    (0, 93), (0, 15, 1), (0, 21, 4), (0, 71), (0, 105), (0, 13, 2, 1), (0, 112), (0, 102), (0, 26), (0, 57,
    3), (0, 121, 1), (0, 72), (0, 48, 0), (0, 38, 0), (0, 69), (0, 41, 0), (0, 62, 3), (0, 106, 2), (0, 84,
    5), (0, 91), (0, 117), (0, 10, 2, 0), (0, 19), (0, 66), (0, 119), (0, 47, 0), (0, 55, 3), (0, 76), (0,
    111, 2), (0, 94), (0, 45), (0, 17, 1), (0, 122, 1, 3), (0, 75, 5), (0, 109), (0, 110, 2, 1), (0, 53, 3,
    0), (0, 80, 4), (0, 89), (0, 14, 2), (0, 87), (0, 58, 3), (0, 22), (0, 70), (0, 113), (0, 115, 1), (0, 51,
    5), (0, 73, 2), (0, 90, 3), (0, 114, 1), (0, 118), (0, 74), (0, 42, 2), (0, 78), (0, 18), (0, 49), (0,
    81), (0, 79), (0, 83), (0, 54), (0, 77), (0, 85), (0, 82), (0, 50), (0, 86), (0, 46),
)

beta_one = 0.9
beta_two = 0.95
learning_rate = 0.05
weight_decay = 0.1
epsilon = 1e-08
correct_one = 1.0 - 0.9**10
correct_two = 1.0 - 0.95**10


def moved(cell, direction):
    x, z, y = cell // 32, cell // 4 % 8, cell % 4
    a, b, c = STEPS[direction]
    return ((x + a) % NX * 8 + (z + b) % NZ) * 4 + (y + c) % NY


def adamw_step(master, first, second, grad_float):
    new_first = beta_one * first + (1.0 - beta_one) * grad_float
    new_second = beta_two * second + (1.0 - beta_two) * grad_float * grad_float
    update = new_first / correct_one / (jnp.sqrt(new_second / correct_two) + epsilon)
    new_master = master - learning_rate * (update + weight_decay * master)
    return (new_master, new_first, new_second)


def gather_kernel(
    failed_at, holder_hbm, ckpt_hbm, master_hbm, first_hbm, second_hbm, grad_hbm,
    weights, master_out, first_out, second_out,
    gathered, ckpt, state, grad, restored, send, recv, holder,
    load_sem, ex_send, ex_recv, ag_send, ag_recv,
):
    dp = lax.axis_index("dp")
    grp = lax.axis_index("grp")
    x, z, y = dp // 32, lax.rem(dp // 4, 8), lax.rem(dp, 4)

    x_at = [lax.rem(x - d + NX, NX) * 32 for d in range(NX)]
    z_at = [lax.rem(z - d + NZ, NZ) * 4 for d in range(NZ)]
    y_at = [lax.rem(y - d + NY, NY) for d in range(NY)]
    shard_at = [x_at[cell // 32] + z_at[cell // 4 % 8] + y_at[cell % 4] for cell in range(128)]
    neighbours = [(shard_at[(-a % NX * 8 + -b % NZ) * 4 + -c % NY], grp) for a, b, c in STEPS]
    peers = [(dp, lax.rem(grp + k, 4)) for k in (1, 2, 3)]

    loads = [
        pltpu.make_async_copy(src, dst, load_sem.at[i])
        for i, (src, dst) in enumerate(
            (
                *((ckpt_hbm.at[:, pl.ds(4 * p, 4)], ckpt.at[:, pl.ds(4 * p, 4)]) for p in range(PARTS)),
                (master_hbm, state.at[0]), (first_hbm, state.at[1]), (second_hbm, state.at[2]),
                (grad_hbm, grad), (holder_hbm, holder),
            )
        )
    ]
    for load in loads:
        load.start()

    barrier = pltpu.get_barrier_semaphore()
    for device in neighbours + peers:
        pl.semaphore_signal(barrier, inc=1, device_id=device, device_id_type=MESH)

    odd = lax.rem(grp, 2) == 1
    sends_near = jnp.logical_or(odd, failed_at[0] == lax.rem(grp + 3, 4))

    def part_copy(src, o, part, kind, device):
        return pltpu.make_async_remote_copy(
            src_ref=src.at[pl.ds(4 * part, 4)],
            dst_ref=recv.at[o, pl.ds(4 * part, 4)],
            send_sem=ex_send.at[PARTS * kind + part],
            recv_sem=ex_recv.at[PARTS * o + part],
            device_id=device,
            device_id_type=MESH,
        )

    first_copies = [part_copy(send.at[0], 0, part, 0, peers[2]) for part in range(PARTS)]
    far_copies = [part_copy(send.at[1], 1, part, 1, peers[1]) for part in range(PARTS)]
    onward_copies = [part_copy(recv.at[0], 1, part, 2, peers[2]) for part in range(PARTS)]
    for part in range(PARTS):
        loads[part].wait()
        for s in range(4 * part, 4 * part + 4):
            for k in range(3):
                near = ckpt[k, s, pl.ds(0, 16, stride=2), :].astype(jnp.bfloat16)
                far = ckpt[k, s, pl.ds(1, 16, stride=2), :].astype(jnp.bfloat16)
                send[0, s, k] = jnp.where(sends_near, near, far)
                send[1, s, k] = far
        if part == 0:
            pl.semaphore_wait(barrier, len(neighbours) + len(peers))
        first_copies[part].start()
        pl.when(odd)(far_copies[part].start)
    for load in loads[PARTS:]:
        load.wait()

    places = []
    seen_near = jnp.int32(0)
    for b in range(16):
        near = holder[0, b] == 1
        places.append((jnp.where(near, 0, 1), jnp.minimum(jnp.where(near, seen_near, b - seen_near), 11)))
        seen_near = seen_near + jnp.where(near, 1, 0)
    failed = failed_at[0] == grp
    for part in range(PARTS):
        first_copies[part].wait_recv()
        pl.when(odd)(onward_copies[part].start)
    for copy in far_copies:
        copy.wait_recv()
    for b, (o, s) in enumerate(places):
        for k in range(3):
            restored[k, pl.ds(64 * (b % 4) + b // 4, 16, stride=4), :] = recv[o, s, k].astype(jnp.float32)
    chosen = [jnp.where(failed, restored[k], state[k]) for k in range(3)]
    new_master, new_first, new_second = adamw_step(*chosen, grad[...].astype(jnp.float32))
    gathered[dp] = new_master.astype(jnp.bfloat16)

    def shard_copy(cell, arrives, direction):
        place = gathered.at[shard_at[cell]]
        return pltpu.make_async_remote_copy(
            src_ref=place,
            dst_ref=place,
            send_sem=ag_send,
            recv_sem=ag_recv.at[arrives],
            device_id=neighbours[direction],
            device_id_type=MESH,
        )

    def place_rows(t):

        for j in range(16):
            shards = [gathered[4 * t + k, 16 * j : 16 * j + 16, :].astype(jnp.float32) for k in range(4)]
            for c in range(4):
                tile = jnp.concatenate([shard[4 * c : 4 * c + 4] for shard in shards], axis=0)
                lanes = 512 * j + 128 * c
                weights[pl.ds(pl.multiple_of(16 * t, 16), 16), lanes : lanes + 128] = tile.astype(jnp.bfloat16)

    def place_lot(low, count):
        def place(i, carry):
            place_rows(i // count * 8 + lax.rem(z + i % count + low, NZ))
            return carry

        lax.fori_loop(0, NX * count, place, 0)

    def in_lot(cell, low, count):
        return (-(cell // 4 % 8) - low) % NZ < count

    lots = [(6, 5), (5, 1), (3, 1), (4, 1)]
    started = max(i for i, (_, _, *directions) in enumerate(TREE) if directions)
    started = max(started, max(i for i, (_, cell, *_) in enumerate(TREE) if in_lot(cell, *lots[0])))
    for _, cell, *directions in TREE[: started + 1]:
        if cell:
            shard_copy(cell, cell, 0).wait_recv()
        for direction in directions:
            shard_copy(cell, moved(cell, direction), direction).start()
        if not cell:
            master_out[...] = new_master
            first_out[...] = new_first
            second_out[...] = new_second
            for copy in first_copies:
                copy.wait_send()

            @pl.when(odd)
            def _():
                for copy in far_copies + onward_copies:
                    copy.wait_send()
    place_lot(*lots[0])
    for lot in lots[1:]:
        for _, cell in TREE[started + 1 :]:
            if in_lot(cell, *lot):
                shard_copy(cell, cell, 0).wait_recv()
        place_lot(*lot)
    everything = gathered.at[pl.ds(0, 127)]
    pltpu.make_async_remote_copy(
        src_ref=everything, dst_ref=everything, send_sem=ag_send, recv_sem=ag_recv.at[0],
        device_id=neighbours[0], device_id_type=MESH,
    ).wait_send()


def output_kernel(*refs):
    copies = [pltpu.make_async_copy(refs[i], refs[i + 4], refs[8].at[i]) for i in range(3)]
    for i in range(8):
        rows = pl.ds(512 // 8 * i, 512 // 8)
        copies.append(pltpu.make_async_copy(refs[3].at[rows], refs[7].at[rows], refs[8].at[3 + i]))
    for copy in copies:
        copy.start()
    for copy in copies:
        copy.wait()


def tiles(rows):
    return rows.reshape(4, 64, 128).transpose(1, 0, 2).reshape(256, 128)


def rows_of(tiled):
    return tiled.reshape(64, 4, 128).transpose(1, 0, 2).reshape(1, 4, 8192)


def per_device(master, first_moment, second_moment, gradient, checkpoints, block_holder, failed_member):
    held = checkpoints.reshape(3, 2, 12, 16, 128).transpose(0, 2, 3, 1, 4).reshape(3, 12, 32, 128)
    operands = [block_holder.reshape(1, 16), held]
    operands += [tiles(value) for value in (master, first_moment, second_moment, gradient)]
    operands = [pltpu.with_memory_space_constraint(value, pltpu.HBM) for value in operands]
    shard = ((256, 128), jnp.float32)
    weights, new_master, new_first, new_second = pl.pallas_call(
        gather_kernel,
        out_shape=[pltpu.VMEM((512, 8192), jnp.bfloat16)] + [pltpu.VMEM(*shard)] * 3,
        in_specs=[pl.BlockSpec(memory_space=pltpu.SMEM)] + [pl.BlockSpec(memory_space=pltpu.HBM)] * 6,
        out_specs=[pl.BlockSpec(memory_space=pltpu.VMEM)] * 4,
        scratch_shapes=[
            pltpu.VMEM((128, 256, 128), jnp.bfloat16),
            pltpu.VMEM((3, 12, 32, 128), jnp.float32),
            pltpu.VMEM((3, 256, 128), jnp.float32),
            pltpu.VMEM((256, 128), jnp.bfloat16),
            pltpu.VMEM((3, 256, 128), jnp.float32),
            pltpu.VMEM((2, 12, 3, 16, 128), jnp.bfloat16),
            pltpu.VMEM((2, 12, 3, 16, 128), jnp.bfloat16),
            pltpu.SMEM((1, 16), jnp.int32),
            pltpu.SemaphoreType.DMA((PARTS + 5,)),
            pltpu.SemaphoreType.DMA((3 * PARTS,)),
            pltpu.SemaphoreType.DMA((2 * PARTS,)),
            pltpu.SemaphoreType.DMA,
            pltpu.SemaphoreType.DMA((128,)),
        ],
        compiler_params=pltpu.CompilerParams(
            collective_id=0, has_side_effects=True, vmem_limit_bytes=24 * 2**20
        ),
        name="restore_step_gather",
    )(failed_member, *operands)
    results = [
        pltpu.with_memory_space_constraint(value, pltpu.VMEM) for value in (new_master, new_first, new_second, weights)
    ]
    new_master, new_first, new_second, weights = pl.pallas_call(
        output_kernel,
        out_shape=[jax.ShapeDtypeStruct(*shard)] * 3 + [jax.ShapeDtypeStruct((512, 8192), jnp.bfloat16)],
        in_specs=[pl.BlockSpec(memory_space=pltpu.VMEM)] * 4,
        out_specs=[pl.BlockSpec(memory_space=pl.ANY)] * 4,
        scratch_shapes=[pltpu.SemaphoreType.DMA((3 + 8,))],
        compiler_params=pltpu.CompilerParams(vmem_limit_bytes=4 * 2**20),
        name="write_outputs",
    )(*results)
    return (rows_of(new_master), rows_of(new_first), rows_of(new_second), weights.reshape(1, 512, 8192))


def solution(mesh):
    return jax.shard_map(
        per_device,
        mesh=mesh,
        in_specs=(
            P("grp", "dp", None),
            P("grp", "dp", None),
            P("grp", "dp", None),
            P("grp", "dp", None),
            P(None, "grp", "dp", None, None, None),
            P("grp", "dp", None),
            P("dp"),
        ),
        out_specs=(
            P("grp", "dp", None),
            P("grp", "dp", None),
            P("grp", "dp", None),
            P("grp", None, None),
        ),
        check_vma=False,
    )
```

time: 71.6 us -> 67.1 us (0.937)
  the two profiles are of different devices: /device:TPU:9 before, /device:TPU:16 now
where the time goes in v3:
time: 67.1 us; the launch traced here: 66.9 us
  Pallas kernels  65.6 us (98%)
  between operations  1.29 us (2%)
    pallas_call x1, Pallas kernels, per_device(): pl.pallas_call(gather_kernel, out_shape=[pltpu.VMEM((512, 8192), jnp.bflo...  62.1 us
    pallas_call x1, Pallas kernels, per_device(): pl.pallas_call(output_kernel, out_shape=[jax.ShapeDtypeStruct(*shard)] *...  3.52 us

profile of v3, /device:TPU:16, one launch (start us, length us, event | category | flops | bytes accessed | tf_op | source)
XLA Modules:
  0.0 66.9 jit_solution(14091409229087985551)
XLA Ops:
  1.3 62.1 %restore_step_gather.1 = (bf16[512,8192]{1,0:T(8,128)(2,1)S(1)}, f32[256,128]{1,0:T(8,128)S(1)}, f32[256,128]{1,0:T(8,128)S(1)}, f32[256,128]{1,0:T(8,128)S(1)}) custom-call(s32[1]{0:T(128)S(6)} %copy.19.failed_at, s32[1,16]{1,0:T(1,128)} %bitcast.47, f32[3,12,32,128]{3,2,1,0:T(8,128)} %bitcast.42, f32[256,128]{1,0:T(8,128)} %bitcast.43, ...), custom_call_target="tpu_custom_call" | custom-call | tf_op jit(solution)/shard_map/restore_step_gather/pallas_call | solution.py:227
  63.4 3.5 %write_outputs.1 = (f32[256,128]{1,0:T(8,128)}, f32[256,128]{1,0:T(8,128)}, f32[256,128]{1,0:T(8,128)}, bf16[512,8192]{1,0:T(8,128)(2,1)}) custom-call(f32[256,128]{1,0:T(8,128)S(1)} %get-tuple-element.12.refs_0_, f32[256,128]{1,0:T(8,128)S(1)} %get-tuple-element.13.refs_1_, f32[256,128]{1,0:T(8,128)S(1)} %get-tuple-element.14.refs_2_, ...), custom_call_target="tpu_custom_call" | custom-call | tf_op jit(solution)/shard_map/write_outputs/pallas_call | solution.py:255

commit v4 on v3

--- a/solution.py
+++ b/solution.py
@@ -16,18 +16,18 @@
     (0, 0, 5, 4, 3, 2, 1, 0), (0, 28, 3, 0, 1), (0, 4, 2, 1, 0), (0, 96, 1, 5), (0, 32, 4), (0, 3, 2, 5, 3,
     0), (0, 1, 3, 2, 1), (0, 24, 3, 0), (0, 60, 0, 4, 5), (0, 124, 3), (0, 8, 4, 0, 2), (0, 36), (0, 100, 2),
     (0, 7, 1, 2, 0), (0, 31, 1, 3, 5), (0, 99), (0, 33), (0, 35, 0), (0, 64, 2, 4), (0, 5, 0), (0, 29, 1, 3),
-    (0, 56, 5), (0, 97, 2), (0, 12, 1), (0, 20, 0, 1, 3), (0, 2, 2, 0, 1), (0, 92, 3), (0, 103, 2, 5), (0,
-    61), (0, 104), (0, 120), (0, 40, 2), (0, 127, 1, 3), (0, 11, 2, 0), (0, 27, 3), (0, 39, 0), (0, 125, 4,
-    1), (0, 63), (0, 9, 2, 1), (0, 68, 2), (0, 25, 0, 3, 1, 4), (0, 67), (0, 108), (0, 101, 1), (0, 16), (0,
-    37, 2), (0, 116, 3, 4), (0, 6, 2, 0), (0, 30), (0, 88), (0, 65), (0, 52, 3, 0), (0, 98), (0, 107, 5), (0,
-    123, 1), (0, 34, 3, 0), (0, 95, 5), (0, 44, 4, 0), (0, 23, 3, 1), (0, 59, 3), (0, 126, 3), (0, 43, 2, 0),
-    (0, 93), (0, 15, 1), (0, 21, 4), (0, 71), (0, 105), (0, 13, 2, 1), (0, 112), (0, 102), (0, 26), (0, 57,
-    3), (0, 121, 1), (0, 72), (0, 48, 0), (0, 38, 0), (0, 69), (0, 41, 0), (0, 62, 3), (0, 106, 2), (0, 84,
-    5), (0, 91), (0, 117), (0, 10, 2, 0), (0, 19), (0, 66), (0, 119), (0, 47, 0), (0, 55, 3), (0, 76), (0,
-    111, 2), (0, 94), (0, 45), (0, 17, 1), (0, 122, 1, 3), (0, 75, 5), (0, 109), (0, 110, 2, 1), (0, 53, 3,
-    0), (0, 80, 4), (0, 89), (0, 14, 2), (0, 87), (0, 58, 3), (0, 22), (0, 70), (0, 113), (0, 115, 1), (0, 51,
-    5), (0, 73, 2), (0, 90, 3), (0, 114, 1), (0, 118), (0, 74), (0, 42, 2), (0, 78), (0, 18), (0, 49), (0,
-    81), (0, 79), (0, 83), (0, 54), (0, 77), (0, 85), (0, 82), (0, 50), (0, 86), (0, 46),
+    (0, 56, 5), (0, 97, 2), (0, 20, 0, 1, 3), (0, 12, 1), (0, 2, 2, 0, 1), (0, 92, 3), (0, 103, 2, 5), (0,
+    120), (0, 104), (0, 61), (0, 40, 2), (0, 127, 1, 3), (0, 27, 3), (0, 11, 2, 0), (0, 39, 0), (0, 63), (0,
+    125, 4, 1), (0, 25, 0, 3, 1, 4), (0, 68, 2), (0, 9, 2, 1), (0, 67), (0, 116, 3, 4), (0, 16), (0, 101, 1),
+    (0, 37, 2), (0, 108), (0, 30), (0, 88), (0, 6, 2, 0), (0, 65), (0, 52, 3, 0), (0, 98), (0, 123, 1), (0,
+    107, 5), (0, 34, 3, 0), (0, 95, 5), (0, 23, 3, 1), (0, 44, 4, 0), (0, 59, 3), (0, 43, 2, 0), (0, 126, 3),
+    (0, 93), (0, 21, 4), (0, 15, 1), (0, 71), (0, 121, 1), (0, 112), (0, 72), (0, 102), (0, 57, 3), (0, 105),
+    (0, 26), (0, 48, 0), (0, 13, 2, 1), (0, 38, 0), (0, 69), (0, 62, 3), (0, 41, 0), (0, 106, 2), (0, 84, 5),
+    (0, 91), (0, 19), (0, 10, 2, 0), (0, 117), (0, 66), (0, 119), (0, 55, 3), (0, 47, 0), (0, 76), (0, 94),
+    (0, 111, 2), (0, 122, 1, 3), (0, 17, 1), (0, 45), (0, 75, 5), (0, 89), (0, 53, 3, 0), (0, 110, 2, 1), (0,
+    80, 4), (0, 109), (0, 58, 3), (0, 14, 2), (0, 87), (0, 22), (0, 70), (0, 90, 3), (0, 51, 5), (0, 115, 1),
+    (0, 73, 2), (0, 113), (0, 118), (0, 114, 1), (0, 42, 2), (0, 78), (0, 49), (0, 74), (0, 18), (0, 79), (0,
+    54), (0, 81), (0, 83), (0, 77), (0, 85), (0, 86), (0, 82), (0, 50), (0, 46),
 )
 
 beta_one = 0.9
@@ -48,7 +48,7 @@
 def adamw_step(master, first, second, grad_float):
     new_first = beta_one * first + (1.0 - beta_one) * grad_float
     new_second = beta_two * second + (1.0 - beta_two) * grad_float * grad_float
-    update = new_first / correct_one / (jnp.sqrt(new_second / correct_two) + epsilon)
+    update = new_first * (1.0 / correct_one) / (jnp.sqrt(new_second * (1.0 / correct_two)) + epsilon)
     new_master = master - learning_rate * (update + weight_decay * master)
     return (new_master, new_first, new_second)
 
@@ -80,12 +80,13 @@
             )
         )
     ]
-    for load in loads:
-        load.start()
+    loads[0].start()
 
     barrier = pltpu.get_barrier_semaphore()
     for device in neighbours + peers:
         pl.semaphore_signal(barrier, inc=1, device_id=device, device_id_type=MESH)
+    for load in loads[1:]:
+        load.start()
 
     odd = lax.rem(grp, 2) == 1
     sends_near = jnp.logical_or(odd, failed_at[0] == lax.rem(grp + 3, 4))

time: 67.1 us -> 67 us (level)
  no operation moved by 1% of the time
where the time goes in v4:
time: 67 us; the launch traced here: 66.9 us
  Pallas kernels  65.6 us (98%)
  between operations  1.29 us (2%)
    pallas_call x1, Pallas kernels, per_device(): pl.pallas_call(gather_kernel, out_shape=[pltpu.VMEM((512, 8192), jnp.bflo...  62.1 us
    pallas_call x1, Pallas kernels, per_device(): pl.pallas_call(output_kernel, out_shape=[jax.ShapeDtypeStruct(*shard)] *...  3.52 us

profile of v4, /device:TPU:16, one launch (start us, length us, event | category | flops | bytes accessed | tf_op | source)
XLA Modules:
  0.0 66.9 jit_solution(744124940978547428)
XLA Ops:
  1.3 62.1 %restore_step_gather.1 = (bf16[512,8192]{1,0:T(8,128)(2,1)S(1)}, f32[256,128]{1,0:T(8,128)S(1)}, f32[256,128]{1,0:T(8,128)S(1)}, f32[256,128]{1,0:T(8,128)S(1)}) custom-call(s32[1]{0:T(128)S(6)} %copy.19.failed_at, s32[1,16]{1,0:T(1,128)} %bitcast.47, f32[3,12,32,128]{3,2,1,0:T(8,128)} %bitcast.42, f32[256,128]{1,0:T(8,128)} %bitcast.43, ...), custom_call_target="tpu_custom_call" | custom-call | tf_op jit(solution)/shard_map/restore_step_gather/pallas_call | solution.py:228
  63.4 3.5 %write_outputs.1 = (f32[256,128]{1,0:T(8,128)}, f32[256,128]{1,0:T(8,128)}, f32[256,128]{1,0:T(8,128)}, bf16[512,8192]{1,0:T(8,128)(2,1)}) custom-call(f32[256,128]{1,0:T(8,128)S(1)} %get-tuple-element.12.refs_0_, f32[256,128]{1,0:T(8,128)S(1)} %get-tuple-element.13.refs_1_, f32[256,128]{1,0:T(8,128)S(1)} %get-tuple-element.14.refs_2_, ...), custom_call_target="tpu_custom_call" | custom-call | tf_op jit(solution)/shard_map/write_outputs/pallas_call | solution.py:256
